TPU v7x, 32 devices: a whole 2x2x4 slice. The times are simulated.
32 devices in a mesh: ctx: 8 (over z, x), pp: 4 (over y, core).
Axes of the slice: x: 2, y: 2, z: 4, core: 2. Of those that a mesh axis runs over, the one named last changes fastest.
Arguments:
- tokens: bfloat16 [1, 1024, 2048], P(None, 'ctx'), may hold values from -6 to 6
- doc_lengths: int32 [4], replicated, may hold values from 1 to 512, 1024 in all
- norm_gain: bfloat16 [4, 2048], P('pp'), may hold values from 0.25 to 1.75
- w_query: bfloat16 [4, 2048, 2048], P('pp'), as said below
- w_key: bfloat16 [4, 2048, 512], P('pp'), as said below
- w_value: bfloat16 [4, 2048, 512], P('pp'), may hold values from -0.125 to 0.125
- w_output: bfloat16 [4, 2048, 2048], P('pp'), may hold values from -0.125 to 0.125
Outputs:
- section_states: bfloat16 [4, 1, 1024, 2048], P('pp', None, 'ctx')
Inputs may be any that keep to these rules, and one draw needn't show every extreme that they name: `doc_lengths`: document lengths sum to 1024; the longest is exactly 512. `w_query`: entries lie within 6 / sqrt(2048) of zero. `w_key`: entries lie within 6 / sqrt(2048) of zero.
All inputs are finite; a program needn't handle non-finite values.
Results may differ from a plain program's by a relative error of at most 0.014.
The roundings to bfloat16 on the way count: a program that leaves them out, or rounds other values in their place, can miss the bound.
Values may be sent and summed in bfloat16 or wider, within the bound.
A program may use at most 192 MiB of HBM per device.

v0:
```python
import functools

import jax
import jax.numpy as jnp
from jax import lax
from jax.experimental import pallas as pl
from jax.experimental.pallas import tpu as pltpu
from jax.sharding import PartitionSpec as P

HD = 128
THETA = 500000.0
EPSILON = 1e-05
NEG_LARGE = -1e30
MESH = pl.DeviceIdType.MESH


def tables(position, lengths):
    order = jnp.arange(lengths.shape[0], dtype=jnp.int32)
    ends = jnp.sum(jnp.where(order[None, :] <= order[:, None], lengths[None, :], 0), axis=1)
    before = ends[None, :] <= position[:, None]
    starts = jnp.sum(jnp.where(before, lengths[None, :], 0), axis=1)
    offsets = position - starts
    half = HD // 2
    freqs = THETA ** (-(jnp.arange(half, dtype=jnp.float32) * 2.0 / HD))
    angles = offsets.astype(jnp.float32)[:, None] * freqs[None, :]
    cosine, sine = jnp.cos(angles), jnp.sin(angles)
    return (
        offsets[:, None],
        jnp.concatenate([cosine, cosine], axis=-1),
        jnp.concatenate([-sine, sine], axis=-1),
    )


def kernel(
    spans,
    sections,
    reach,
    tok_ref,
    off_ref,
    cos_ref,
    sin_ref,
    gain_ref,
    wq_ref,
    wk_ref,
    wv_ref,
    wo_ref,
    out_ref,
    wq,
    wk,
    wv,
    wo,
    hid,
    normed,
    queries,
    kv,
    att,
    bias,
    w_sem,
    kv_send,
    kv_recv,
    hid_send,
    hid_recv,
):
    me = lax.axis_index("ctx")
    seg = lax.axis_index("pp")
    rows, width = tok_ref.shape
    groups, part = wq.shape[0], wq.shape[2]
    chunks, piece = hid.shape[0], hid.shape[2]
    kv_width = wk.shape[1]
    heads_in = part // HD

    loads = [
        pltpu.make_async_copy(wk_ref, wk, w_sem.at[0]),
        pltpu.make_async_copy(wv_ref, wv, w_sem.at[1]),
    ]
    for g in range(groups):
        loads.append(
            pltpu.make_async_copy(wq_ref.at[:, pl.ds(g * part, part)], wq.at[g], w_sem.at[2 + g])
        )
    for c in range(chunks):
        loads.append(
            pltpu.make_async_copy(
                wo_ref.at[:, pl.ds(c * piece, piece)], wo.at[c], w_sem.at[2 + groups + c]
            )
        )
    for load in loads:
        load.start()

    barrier = pltpu.get_barrier_semaphore()
    partners = []
    for d in range(1, reach + 1):
        partners.append((me >= d, {"ctx": me - d}))
        partners.append((me + d < spans, {"ctx": me + d}))
    partners.append((seg >= 1, {"pp": seg - 1}))
    partners.append((seg + 1 < sections, {"pp": seg + 1}))
    for there, where in partners:

        @pl.when(there)
        def _(where=where):
            pl.semaphore_signal(barrier, inc=1, device_id=where, device_id_type=MESH)

    for d in range(1, reach + 1):

        @pl.when(me < d)
        def _(d=d):
            kv[reach - d] = jnp.zeros(kv.shape[1:], kv.dtype)

    offset = off_ref[...]
    row = lax.broadcasted_iota(jnp.int32, (rows, rows), 0)
    col = lax.broadcasted_iota(jnp.int32, (rows, rows), 1)
    for d in range(reach + 1):
        gap = row - col + d * rows
        bias[:, pl.ds((reach - d) * rows, rows)] = jnp.where(
            (gap >= 0) & (gap <= offset), 0.0, NEG_LARGE
        )

    peers = sum(there.astype(jnp.int32) for there, where in partners)
    pl.semaphore_wait(barrier, peers)

    def hand_over(c, device):
        return pltpu.make_async_remote_copy(
            src_ref=out_ref.at[:, pl.ds(c * piece, piece)],
            dst_ref=hid.at[c],
            send_sem=hid_send.at[c],
            recv_sem=hid_recv.at[c],
            device_id={"pp": device},
            device_id_type=MESH,
        )

    def spread(d, device):
        return pltpu.make_async_remote_copy(
            src_ref=kv.at[reach],
            dst_ref=kv.at[reach - d],
            send_sem=kv_send.at[d - 1],
            recv_sem=kv_recv.at[d - 1],
            device_id={"ctx": device},
            device_id_type=MESH,
        )

    @pl.when(seg == 0)
    def _():
        for c in range(chunks):
            hid[c] = tok_ref[:, c * piece : (c + 1) * piece]

    @pl.when(seg >= 1)
    def _():
        for c in range(chunks):
            hand_over(c, seg - 1).wait_recv()

    square = jnp.zeros((rows, 1), jnp.float32)
    for c in range(chunks):
        wide = hid[c].astype(jnp.float32)
        square += jnp.sum(wide * wide, axis=-1, keepdims=True)
    inverse = lax.rsqrt(square / width + EPSILON)
    for c in range(chunks):
        at = slice(c * piece, (c + 1) * piece)
        gain = gain_ref[:, at].astype(jnp.float32)
        normed[:, at] = (hid[c].astype(jnp.float32) * inverse * gain).astype(jnp.bfloat16)

    def turn(head):
        return (head * cos_ref[...] + pltpu.roll(head, HD // 2, 1) * sin_ref[...]).astype(
            jnp.bfloat16
        )

    loads[0].wait()
    keys = jnp.dot(normed[...], wk[...], preferred_element_type=jnp.float32)
    for g in range(groups):
        kv[reach, :, g * HD : (g + 1) * HD] = turn(keys[:, g * HD : (g + 1) * HD])
    loads[1].wait()
    kv[reach, :, kv_width : 2 * kv_width] = jnp.dot(
        normed[...], wv[...], preferred_element_type=jnp.float32
    ).astype(jnp.bfloat16)

    for d in range(1, reach + 1):

        @pl.when(me + d < spans)
        def _(d=d):
            spread(d, me + d).start()

    for g in range(groups):
        loads[2 + g].wait()

    @pl.loop(0, groups)
    def _(g):
        block = jnp.dot(normed[...], wq[g], preferred_element_type=jnp.float32)
        for j in range(heads_in):
            queries[g, j * rows : (j + 1) * rows] = turn(block[:, j * HD : (j + 1) * HD])

    for d in range(1, reach + 1):

        @pl.when(me >= d)
        def _(d=d):
            spread(d, me - d).wait_recv()

    count = (reach + 1) * rows

    @pl.loop(0, groups)
    def _(g):
        k_at = pl.ds(pl.multiple_of(g * HD, HD), HD)
        v_at = pl.ds(pl.multiple_of(kv_width + g * HD, HD), HD)
        ks = kv[:, :, k_at].reshape(count, HD)
        vs = kv[:, :, v_at].reshape(count, HD)
        for j in range(heads_in):
            scores = lax.dot_general(
                queries[g, j * rows : (j + 1) * rows],
                ks,
                (((1,), (1,)), ((), ())),
                preferred_element_type=jnp.float32,
            )
            scores = scores * (HD ** (-0.5)) + bias[...]
            peak = jnp.max(scores, axis=-1, keepdims=True)
            weights = jnp.exp(scores - peak)
            total = jnp.sum(weights, axis=-1, keepdims=True)
            mixed = jnp.dot(weights.astype(jnp.bfloat16), vs, preferred_element_type=jnp.float32)
            at = pl.ds(pl.multiple_of(g * part + j * HD, HD), HD)
            att[:, at] = (mixed / total).astype(jnp.bfloat16)

    for c in range(chunks):
        loads[2 + groups + c].wait()

    @pl.loop(0, chunks)
    def _(c):
        at = pl.ds(pl.multiple_of(c * piece, piece), piece)
        out_ref[:, at] = (
            hid[c].astype(jnp.float32)
            + jnp.dot(att[...], wo[c], preferred_element_type=jnp.float32)
        ).astype(jnp.bfloat16)

        @pl.when(seg + 1 < sections)
        def _():
            pltpu.make_async_remote_copy(
                src_ref=out_ref.at[:, at],
                dst_ref=hid.at[c],
                send_sem=hid_send.at[c],
                recv_sem=hid_recv.at[c],
                device_id={"pp": seg + 1},
                device_id_type=MESH,
            ).start()

    for d in range(1, reach + 1):

        @pl.when(me + d < spans)
        def _(d=d):
            spread(d, me + d).wait_send()

    @pl.when(seg + 1 < sections)
    def _():
        for c in range(chunks):
            hand_over(c, seg + 1).wait_send()


def solution(mesh):
    spans, sections = mesh.shape["ctx"], mesh.shape["pp"]
    reach = spans // 2

    def per_device(tokens, doc_lengths, norm_gain, w_query, w_key, w_value, w_output):
        rows, width = tokens.shape[1:]
        kv_width = w_key.shape[2]
        groups = kv_width // HD
        part = w_query.shape[2] // groups
        mixed_width = w_output.shape[1]
        chunks = 4
        piece = width // chunks
        position = lax.axis_index("ctx") * rows + jnp.arange(rows, dtype=jnp.int32)
        offsets, cosine, sine = tables(position, doc_lengths)
        vmem = pl.BlockSpec(memory_space=pltpu.VMEM)
        hbm = pl.BlockSpec(memory_space=pl.ANY)
        out = pl.pallas_call(
            functools.partial(kernel, spans, sections, reach),
            out_shape=jax.ShapeDtypeStruct((rows, width), jnp.bfloat16),
            in_specs=[vmem] * 5 + [hbm] * 4,
            out_specs=vmem,
            scratch_shapes=[
                pltpu.VMEM((groups, width, part), jnp.bfloat16),
                pltpu.VMEM((width, kv_width), jnp.bfloat16),
                pltpu.VMEM((width, kv_width), jnp.bfloat16),
                pltpu.VMEM((chunks, mixed_width, piece), jnp.bfloat16),
                pltpu.VMEM((chunks, rows, piece), jnp.bfloat16),
                pltpu.VMEM((rows, width), jnp.bfloat16),
                pltpu.VMEM((groups, part // HD * rows, HD), jnp.bfloat16),
                pltpu.VMEM((reach + 1, rows, 2 * kv_width), jnp.bfloat16),
                pltpu.VMEM((rows, mixed_width), jnp.bfloat16),
                pltpu.VMEM((rows, (reach + 1) * rows), jnp.float32),
                pltpu.SemaphoreType.DMA((2 + groups + chunks,)),
                pltpu.SemaphoreType.DMA((reach,)),
                pltpu.SemaphoreType.DMA((reach,)),
                pltpu.SemaphoreType.DMA((chunks,)),
                pltpu.SemaphoreType.DMA((chunks,)),
            ],
            compiler_params=pltpu.CompilerParams(
                collective_id=0, has_side_effects=True, vmem_limit_bytes=52 << 20
            ),
        )(
            tokens[0],
            offsets,
            cosine,
            sine,
            norm_gain,
            w_query[0],
            w_key[0],
            w_value[0],
            w_output[0],
        )
        return out[None, None]

    in_specs = (
        P(None, "ctx", None),
        P(),
        P("pp", None),
        P("pp", None, None),
        P("pp", None, None),
        P("pp", None, None),
        P("pp", None, None),
    )
    return jax.shard_map(
        per_device,
        mesh=mesh,
        in_specs=in_specs,
        out_specs=P("pp", None, "ctx", None),
        check_vma=False,
    )
```

profile of v0, /device:TPU:31, one launch (start us, length us, event | category | flops | bytes accessed | tf_op | source)
XLA Modules:
  0.0 93.3 jit_solution(17681089039929054199)
XLA Ops:
  0.0 0.8 select_reduce_fusion.1
  0.8 0.7 select_reduce_fusion
  1.5 0.1 copy.11
  1.7 0.3 fusion
  2.0 0.1 pad_maximum_fusion
  2.1 0.0 copy-start
  2.1 1.0 %copy-done = bf16[1,128,2048]{2,1,0:T(8,128)(2,1)S(1)} copy-done((bf16[1,128,2048]{2,1,0:T(8,128)(2,1)S(1)}, bf16[1,128,2048]{2,1,0:T(8,128)(2,1)}, u32[]{:S(2)}) %copy-start) | copy-done | bytes 524312
  3.1 0.0 copy-start.1
  3.1 0.7 copy-done.1
  3.8 88.6 %shard_map.73 = bf16[128,2048]{1,0:T(8,128)(2,1)S(1)} custom-call(bf16[128,2048]{1,0:T(8,128)(2,1)S(1)} %bitcast.8, s32[128,1]{1,0:T(8,128)S(1)} %add_subtract_fusion.off_ref, f32[128,128]{1,0:T(8,128)S(1)} %get-tuple-element.8.cos_ref, f32[128,128]{1,0:T(8,128)S(1)} %get-tuple-element.9.sin_ref, bf16[1,2048]{1,0:T(2,128)(2,1)S(1)} %copy-done.1, ...), custom_call_target="tpu_custom_call" | custom-call | tf_op jit(solution)/shard_map/pallas_call | solution.py:268
  92.5 0.8 copy.13
  (4 shorter events, 0.0 us)
Async XLA Ops:
  2.1 1.0 %copy-start = (bf16[1,128,2048]{2,1,0:T(8,128)(2,1)S(1)}, bf16[1,128,2048]{2,1,0:T(8,128)(2,1)}, u32[]{:S(2)}) copy-start(bf16[1,128,2048]{2,1,0:T(8,128)(2,1)} %param.7) | copy-start | bytes 1572868
  3.1 0.7 copy-start.1
where the time goes:
time: 93.5 us; the launch traced here: 93.3 us
  Pallas kernels  88.6 us (95%)
  local copies, waits for them, and re-layouts  2.64 us (3%)
  other arithmetic  1.95 us (2%)
    pallas_call x1, Pallas kernels, per_device(): pl.pallas_call(functools.partial(kernel, spans, sections, reach), out_sha...  88.6 us
    unnamed x5, local copies, waits for them, and re-layouts  2.53 us

commit v1 on v0

--- a/solution.py
+++ b/solution.py
@@ -56,7 +56,8 @@
     att,
     bias,
     w_sem,
-    kv_send,
+    far_send,
+    near_send,
     kv_recv,
     hid_send,
     hid_recv,
@@ -66,7 +67,6 @@
     rows, width = tok_ref.shape
     groups, part = wq.shape[0], wq.shape[2]
     chunks, piece = hid.shape[0], hid.shape[2]
-    kv_width = wk.shape[1]
     heads_in = part // HD
 
     loads = [
@@ -88,9 +88,11 @@
 
     barrier = pltpu.get_barrier_semaphore()
     partners = []
-    for d in range(1, reach + 1):
-        partners.append((me >= d, {"ctx": me - d}))
-        partners.append((me + d < spans, {"ctx": me + d}))
+    even = lax.rem(me, 2) == 0
+    pair = me + 1 - 2 * lax.rem(me, 2)
+    partners.append((me >= 2, {"ctx": me - 2}))
+    partners.append((me + 2 < spans, {"ctx": me + 2}))
+    partners.append((me >= 0, {"ctx": pair}))
     partners.append((seg >= 1, {"pp": seg - 1}))
     partners.append((seg + 1 < sections, {"pp": seg + 1}))
     for there, where in partners:
@@ -103,7 +105,8 @@
 
         @pl.when(me < d)
         def _(d=d):
-            kv[reach - d] = jnp.zeros(kv.shape[1:], kv.dtype)
+            for t in range(2):
+                kv[t, reach - d] = jnp.zeros(kv.shape[2:], kv.dtype)
 
     offset = off_ref[...]
     row = lax.broadcasted_iota(jnp.int32, (rows, rows), 0)
@@ -127,15 +130,43 @@
             device_id_type=MESH,
         )
 
-    def spread(d, device):
+    def along(t, d, device):
         return pltpu.make_async_remote_copy(
-            src_ref=kv.at[reach],
-            dst_ref=kv.at[reach - d],
-            send_sem=kv_send.at[d - 1],
-            recv_sem=kv_recv.at[d - 1],
+            src_ref=kv.at[t, reach - d],
+            dst_ref=kv.at[t, reach - d - 2],
+            send_sem=far_send.at[t, d // 2],
+            recv_sem=kv_recv.at[t, d + 1],
             device_id={"ctx": device},
             device_id_type=MESH,
         )
+
+    def across(t, d, to):
+        return pltpu.make_async_remote_copy(
+            src_ref=kv.at[t, reach - d],
+            dst_ref=kv.at[t, reach - to],
+            send_sem=near_send.at[t, d // 2],
+            recv_sem=kv_recv.at[t, to - 1],
+            device_id={"ctx": pair},
+            device_id_type=MESH,
+        )
+
+    def routes(d):
+        held = me >= d
+        found = []
+        if d + 2 <= reach:
+            found.append((held & (me + 2 < spans), lambda t: along(t, d, me + 2)))
+        if d + 1 <= reach:
+            found.append((held & even, lambda t: across(t, d, d + 1)))
+        if d >= 2:
+            found.append((held & jnp.logical_not(even), lambda t: across(t, d, d - 1)))
+        return found
+
+    def pass_on(t, d):
+        for open_, copy in routes(d):
+
+            @pl.when(open_)
+            def _(copy=copy):
+                copy(t).start()
 
     @pl.when(seg == 0)
     def _():
@@ -165,17 +196,14 @@
     loads[0].wait()
     keys = jnp.dot(normed[...], wk[...], preferred_element_type=jnp.float32)
     for g in range(groups):
-        kv[reach, :, g * HD : (g + 1) * HD] = turn(keys[:, g * HD : (g + 1) * HD])
+        kv[0, reach, :, g * HD : (g + 1) * HD] = turn(keys[:, g * HD : (g + 1) * HD])
+    pass_on(0, 0)
     loads[1].wait()
-    kv[reach, :, kv_width : 2 * kv_width] = jnp.dot(
+    kv[1, reach] = jnp.dot(
         normed[...], wv[...], preferred_element_type=jnp.float32
     ).astype(jnp.bfloat16)
 
-    for d in range(1, reach + 1):
-
-        @pl.when(me + d < spans)
-        def _(d=d):
-            spread(d, me + d).start()
+    pass_on(1, 0)
 
     for g in range(groups):
         loads[2 + g].wait()
@@ -186,20 +214,29 @@
         for j in range(heads_in):
             queries[g, j * rows : (j + 1) * rows] = turn(block[:, j * HD : (j + 1) * HD])
 
-    for d in range(1, reach + 1):
-
-        @pl.when(me >= d)
-        def _(d=d):
-            spread(d, me - d).wait_recv()
+    for d in range(2, reach + 1, 2):
+        for t in range(2):
+
+            @pl.when(me >= d)
+            def _(d=d, t=t):
+                along(t, d - 2, me - 2).wait_recv()
+
+            pass_on(t, d)
+
+    for d in range(1, reach + 1, 2):
+        for t in range(2):
+
+            @pl.when(me >= d)
+            def _(d=d, t=t):
+                across(t, d - 1, d).wait_recv()
 
     count = (reach + 1) * rows
 
     @pl.loop(0, groups)
     def _(g):
         k_at = pl.ds(pl.multiple_of(g * HD, HD), HD)
-        v_at = pl.ds(pl.multiple_of(kv_width + g * HD, HD), HD)
-        ks = kv[:, :, k_at].reshape(count, HD)
-        vs = kv[:, :, v_at].reshape(count, HD)
+        ks = kv[0, :, :, k_at].reshape(count, HD)
+        vs = kv[1, :, :, k_at].reshape(count, HD)
         for j in range(heads_in):
             scores = lax.dot_general(
                 queries[g, j * rows : (j + 1) * rows],
@@ -237,11 +274,13 @@
                 device_id_type=MESH,
             ).start()
 
-    for d in range(1, reach + 1):
-
-        @pl.when(me + d < spans)
-        def _(d=d):
-            spread(d, me + d).wait_send()
+    for d in range(0, reach + 1, 2):
+        for t in range(2):
+            for open_, copy in routes(d):
+
+                @pl.when(open_)
+                def _(copy=copy, t=t):
+                    copy(t).wait_send()
 
     @pl.when(seg + 1 < sections)
     def _():
@@ -278,12 +317,13 @@
                 pltpu.VMEM((chunks, rows, piece), jnp.bfloat16),
                 pltpu.VMEM((rows, width), jnp.bfloat16),
                 pltpu.VMEM((groups, part // HD * rows, HD), jnp.bfloat16),
-                pltpu.VMEM((reach + 1, rows, 2 * kv_width), jnp.bfloat16),
+                pltpu.VMEM((2, reach + 1, rows, kv_width), jnp.bfloat16),
                 pltpu.VMEM((rows, mixed_width), jnp.bfloat16),
                 pltpu.VMEM((rows, (reach + 1) * rows), jnp.float32),
                 pltpu.SemaphoreType.DMA((2 + groups + chunks,)),
-                pltpu.SemaphoreType.DMA((reach,)),
-                pltpu.SemaphoreType.DMA((reach,)),
+                pltpu.SemaphoreType.DMA((2, reach // 2 + 1)),
+                pltpu.SemaphoreType.DMA((2, reach // 2 + 1)),
+                pltpu.SemaphoreType.DMA((2, reach)),
                 pltpu.SemaphoreType.DMA((chunks,)),
                 pltpu.SemaphoreType.DMA((chunks,)),
             ],

time: 93.5 us -> 87.5 us (0.936)
  Pallas kernels: 88.6 us -> 82.6 us
    pallas_call x1, Pallas kernels: 88.6 us -> 82.6 us  [per_device(): pl.pallas_call(functools.partial(kernel, spans, sections, reach), out_sha...]
where the time goes in v1:
time: 87.5 us; the launch traced here: 87.3 us
  Pallas kernels  82.6 us (94%)
  local copies, waits for them, and re-layouts  2.64 us (3%)
  other arithmetic  1.95 us (2%)
    pallas_call x1, Pallas kernels, per_device(): pl.pallas_call(functools.partial(kernel, spans, sections, reach), out_sha...  82.6 us
    unnamed x5, local copies, waits for them, and re-layouts  2.53 us

profile of v1, /device:TPU:31, one launch (start us, length us, event | category | flops | bytes accessed | tf_op | source)
XLA Modules:
  0.0 87.3 jit_solution(14738063324763978443)
XLA Ops:
  0.0 0.8 select_reduce_fusion.1
  0.8 0.7 select_reduce_fusion
  1.5 0.1 copy.11
  1.7 0.3 fusion
  2.0 0.1 pad_maximum_fusion
  2.1 0.0 copy-start
  2.1 1.0 %copy-done = bf16[1,128,2048]{2,1,0:T(8,128)(2,1)S(1)} copy-done((bf16[1,128,2048]{2,1,0:T(8,128)(2,1)S(1)}, bf16[1,128,2048]{2,1,0:T(8,128)(2,1)}, u32[]{:S(2)}) %copy-start) | copy-done | bytes 524312
  3.1 0.0 copy-start.1
  3.1 0.7 copy-done.1
  3.8 82.6 %shard_map.73 = bf16[128,2048]{1,0:T(8,128)(2,1)S(1)} custom-call(bf16[128,2048]{1,0:T(8,128)(2,1)S(1)} %bitcast.8, s32[128,1]{1,0:T(8,128)S(1)} %add_subtract_fusion.off_ref, f32[128,128]{1,0:T(8,128)S(1)} %get-tuple-element.8.cos_ref, f32[128,128]{1,0:T(8,128)S(1)} %get-tuple-element.9.sin_ref, bf16[1,2048]{1,0:T(2,128)(2,1)S(1)} %copy-done.1, ...), custom_call_target="tpu_custom_call" | custom-call | tf_op jit(solution)/shard_map/pallas_call | solution.py:307
  86.5 0.8 copy.13
  (4 shorter events, 0.0 us)
Async XLA Ops:
  2.1 1.0 %copy-start = (bf16[1,128,2048]{2,1,0:T(8,128)(2,1)S(1)}, bf16[1,128,2048]{2,1,0:T(8,128)(2,1)}, u32[]{:S(2)}) copy-start(bf16[1,128,2048]{2,1,0:T(8,128)(2,1)} %param.7) | copy-start | bytes 1572868
  3.1 0.7 copy-start.1

commit v2 on v1

--- a/solution.py
+++ b/solution.py
@@ -55,6 +55,9 @@
     kv,
     att,
     bias,
+    peaks,
+    totals,
+    sums,
     w_sem,
     far_send,
     near_send,
@@ -83,7 +86,7 @@
                 wo_ref.at[:, pl.ds(c * piece, piece)], wo.at[c], w_sem.at[2 + groups + c]
             )
         )
-    for load in loads:
+    for load in loads[:2]:
         load.start()
 
     barrier = pltpu.get_barrier_semaphore()
@@ -168,6 +171,14 @@
             def _(copy=copy):
                 copy(t).start()
 
+    for load in loads[2 : 2 + groups]:
+        load.start()
+
+    @pl.when(seg >= 1)
+    def _():
+        for load in loads[2 + groups :]:
+            load.start()
+
     @pl.when(seg == 0)
     def _():
         for c in range(chunks):
@@ -199,6 +210,12 @@
         kv[0, reach, :, g * HD : (g + 1) * HD] = turn(keys[:, g * HD : (g + 1) * HD])
     pass_on(0, 0)
     loads[1].wait()
+
+    @pl.when(seg == 0)
+    def _():
+        for load in loads[2 + groups :]:
+            load.start()
+
     kv[1, reach] = jnp.dot(
         normed[...], wv[...], preferred_element_type=jnp.float32
     ).astype(jnp.bfloat16)
@@ -214,43 +231,73 @@
         for j in range(heads_in):
             queries[g, j * rows : (j + 1) * rows] = turn(block[:, j * HD : (j + 1) * HD])
 
-    for d in range(2, reach + 1, 2):
+    def relay(d, side):
         for t in range(2):
 
+            @pl.when(side & (me >= d))
+            def _(t=t):
+                along(t, d - 2, me - 2).wait_recv()
+                pass_on(t, d)
+
+    def from_pair(d):
+        for t in range(2):
+
             @pl.when(me >= d)
-            def _(d=d, t=t):
-                along(t, d - 2, me - 2).wait_recv()
-
-            pass_on(t, d)
-
-    for d in range(1, reach + 1, 2):
-        for t in range(2):
-
-            @pl.when(me >= d)
-            def _(d=d, t=t):
+            def _(t=t):
                 across(t, d - 1, d).wait_recv()
 
-    count = (reach + 1) * rows
+    def part_of(g, j, first, last):
+        at = pl.ds(pl.multiple_of(g * HD, HD), HD)
+        count = (last - first) * rows
+        scores = lax.dot_general(
+            queries[g, j * rows : (j + 1) * rows],
+            kv[0, first:last, :, at].reshape(count, HD),
+            (((1,), (1,)), ((), ())),
+            preferred_element_type=jnp.float32,
+        )
+        scores = scores * (HD ** (-0.5)) + bias[:, first * rows : last * rows]
+        return scores, kv[1, first:last, :, at].reshape(count, HD)
+
+    near = reach - 2
+    relay(2, me >= 0)
+    for d in range(4, reach + 1, 2):
+        relay(d, jnp.logical_not(even))
+    from_pair(1)
 
     @pl.loop(0, groups)
     def _(g):
-        k_at = pl.ds(pl.multiple_of(g * HD, HD), HD)
-        ks = kv[0, :, :, k_at].reshape(count, HD)
-        vs = kv[1, :, :, k_at].reshape(count, HD)
         for j in range(heads_in):
-            scores = lax.dot_general(
-                queries[g, j * rows : (j + 1) * rows],
-                ks,
-                (((1,), (1,)), ((), ())),
-                preferred_element_type=jnp.float32,
-            )
-            scores = scores * (HD ** (-0.5)) + bias[...]
+            scores, vs = part_of(g, j, near, reach + 1)
             peak = jnp.max(scores, axis=-1, keepdims=True)
             weights = jnp.exp(scores - peak)
             total = jnp.sum(weights, axis=-1, keepdims=True)
-            mixed = jnp.dot(weights.astype(jnp.bfloat16), vs, preferred_element_type=jnp.float32)
-            at = pl.ds(pl.multiple_of(g * part + j * HD, HD), HD)
-            att[:, at] = (mixed / total).astype(jnp.bfloat16)
+            at = slice(j * rows, (j + 1) * rows)
+            peaks[g, at] = jnp.broadcast_to(peak, (rows, HD))
+            totals[g, at] = jnp.broadcast_to(total, (rows, HD))
+            sums[g, at] = jnp.dot(
+                weights.astype(jnp.bfloat16), vs, preferred_element_type=jnp.float32
+            )
+
+    for d in range(4, reach + 1, 2):
+        relay(d, even)
+    for d in range(3, reach + 1, 2):
+        from_pair(d)
+
+    @pl.loop(0, groups)
+    def _(g):
+        for j in range(heads_in):
+            scores, vs = part_of(g, j, 0, near)
+            at = slice(j * rows, (j + 1) * rows)
+            old = peaks[g, at]
+            peak = jnp.maximum(old[:, :1], jnp.max(scores, axis=-1, keepdims=True))
+            weights = jnp.exp(scores - peak)
+            fade = jnp.exp(old - peak)
+            total = totals[g, at] * fade + jnp.sum(weights, axis=-1, keepdims=True)
+            mixed = sums[g, at] * fade + jnp.dot(
+                weights.astype(jnp.bfloat16), vs, preferred_element_type=jnp.float32
+            )
+            to = pl.ds(pl.multiple_of(g * part + j * HD, HD), HD)
+            att[:, to] = (mixed / total).astype(jnp.bfloat16)
 
     for c in range(chunks):
         loads[2 + groups + c].wait()
@@ -320,6 +367,9 @@
                 pltpu.VMEM((2, reach + 1, rows, kv_width), jnp.bfloat16),
                 pltpu.VMEM((rows, mixed_width), jnp.bfloat16),
                 pltpu.VMEM((rows, (reach + 1) * rows), jnp.float32),
+                pltpu.VMEM((groups, part // HD * rows, HD), jnp.float32),
+                pltpu.VMEM((groups, part // HD * rows, HD), jnp.float32),
+                pltpu.VMEM((groups, part // HD * rows, HD), jnp.float32),
                 pltpu.SemaphoreType.DMA((2 + groups + chunks,)),
                 pltpu.SemaphoreType.DMA((2, reach // 2 + 1)),
                 pltpu.SemaphoreType.DMA((2, reach // 2 + 1)),

time: 87.5 us -> 91.6 us (1.047); the launches traced: 87.3 us -> 89.8 us
  Pallas kernels: 82.6 us -> 85.2 us
    pallas_call x1, Pallas kernels: 82.6 us -> 85.2 us  [per_device(): pl.pallas_call(functools.partial(kernel, spans, sections, reach), out_sha...]
where the time goes in v2:
time: 91.6 us; the launch traced here: 89.8 us
  Pallas kernels  85.2 us (93%)
  local copies, waits for them, and re-layouts  2.64 us (3%)
  other arithmetic  1.95 us (2%)
    pallas_call x1, Pallas kernels, per_device(): pl.pallas_call(functools.partial(kernel, spans, sections, reach), out_sha...  85.2 us
    unnamed x5, local copies, waits for them, and re-layouts  2.53 us

profile of v2, /device:TPU:31, one launch (start us, length us, event | category | flops | bytes accessed | tf_op | source)
XLA Modules:
  0.0 89.8 jit_solution(3219776023921465915)
XLA Ops:
  0.0 0.8 select_reduce_fusion.1
  0.8 0.7 select_reduce_fusion
  1.5 0.1 copy.11
  1.7 0.3 fusion
  2.0 0.1 pad_maximum_fusion
  2.1 0.0 copy-start
  2.1 1.0 %copy-done = bf16[1,128,2048]{2,1,0:T(8,128)(2,1)S(1)} copy-done((bf16[1,128,2048]{2,1,0:T(8,128)(2,1)S(1)}, bf16[1,128,2048]{2,1,0:T(8,128)(2,1)}, u32[]{:S(2)}) %copy-start) | copy-done | bytes 524312
  3.1 0.0 copy-start.1
  3.1 0.7 copy-done.1
  3.8 85.2 %shard_map.73 = bf16[128,2048]{1,0:T(8,128)(2,1)S(1)} custom-call(bf16[128,2048]{1,0:T(8,128)(2,1)S(1)} %bitcast.8, s32[128,1]{1,0:T(8,128)S(1)} %add_subtract_fusion.off_ref, f32[128,128]{1,0:T(8,128)S(1)} %get-tuple-element.8.cos_ref, f32[128,128]{1,0:T(8,128)S(1)} %get-tuple-element.9.sin_ref, bf16[1,2048]{1,0:T(2,128)(2,1)S(1)} %copy-done.1, ...), custom_call_target="tpu_custom_call" | custom-call | tf_op jit(solution)/shard_map/pallas_call | solution.py:354
  89.0 0.8 copy.13
  (4 shorter events, 0.0 us)
Async XLA Ops:
  2.1 1.0 %copy-start = (bf16[1,128,2048]{2,1,0:T(8,128)(2,1)S(1)}, bf16[1,128,2048]{2,1,0:T(8,128)(2,1)}, u32[]{:S(2)}) copy-start(bf16[1,128,2048]{2,1,0:T(8,128)(2,1)} %param.7) | copy-start | bytes 1572868
  3.1 0.7 copy-start.1

commit v3 on v1

--- a/solution.py
+++ b/solution.py
@@ -232,25 +232,23 @@
 
     count = (reach + 1) * rows
 
-    @pl.loop(0, groups)
-    def _(g):
-        k_at = pl.ds(pl.multiple_of(g * HD, HD), HD)
-        ks = kv[0, :, :, k_at].reshape(count, HD)
-        vs = kv[1, :, :, k_at].reshape(count, HD)
+    for g in range(groups):
+        at = slice(g * HD, (g + 1) * HD)
+        ks = kv[0, :, :, at].reshape(count, HD)
+        vs = kv[1, :, :, at].reshape(count, HD)
+        scores = lax.dot_general(
+            queries[g], ks, (((1,), (1,)), ((), ())), preferred_element_type=jnp.float32
+        )
+        scores = scores.reshape(heads_in, rows, count) * (HD ** (-0.5)) + bias[...][None]
+        scores = scores.reshape(heads_in * rows, count)
+        peak = jnp.max(scores, axis=-1, keepdims=True)
+        weights = jnp.exp(scores - peak)
+        total = jnp.sum(weights, axis=-1, keepdims=True)
+        mixed = jnp.dot(weights.astype(jnp.bfloat16), vs, preferred_element_type=jnp.float32)
+        mixed = (mixed / total).astype(jnp.bfloat16)
         for j in range(heads_in):
-            scores = lax.dot_general(
-                queries[g, j * rows : (j + 1) * rows],
-                ks,
-                (((1,), (1,)), ((), ())),
-                preferred_element_type=jnp.float32,
-            )
-            scores = scores * (HD ** (-0.5)) + bias[...]
-            peak = jnp.max(scores, axis=-1, keepdims=True)
-            weights = jnp.exp(scores - peak)
-            total = jnp.sum(weights, axis=-1, keepdims=True)
-            mixed = jnp.dot(weights.astype(jnp.bfloat16), vs, preferred_element_type=jnp.float32)
-            at = pl.ds(pl.multiple_of(g * part + j * HD, HD), HD)
-            att[:, at] = (mixed / total).astype(jnp.bfloat16)
+            to = g * part + j * HD
+            att[:, to : to + HD] = mixed[j * rows : (j + 1) * rows]
 
     for c in range(chunks):
         loads[2 + groups + c].wait()

time: 87.5 us -> 76.6 us (0.88)
  Pallas kernels: 82.6 us -> 71.7 us
    pallas_call x1, Pallas kernels: 82.6 us -> 71.7 us  [per_device(): pl.pallas_call(functools.partial(kernel, spans, sections, reach), out_sha...]
where the time goes in v3:
time: 76.6 us; the launch traced here: 76.4 us
  Pallas kernels  71.7 us (94%)
  local copies, waits for them, and re-layouts  2.64 us (3%)
  other arithmetic  1.95 us (3%)
    pallas_call x1, Pallas kernels, per_device(): pl.pallas_call(functools.partial(kernel, spans, sections, reach), out_sha...  71.7 us
    unnamed x5, local copies, waits for them, and re-layouts  2.53 us

profile of v3, /device:TPU:31, one launch (start us, length us, event | category | flops | bytes accessed | tf_op | source)
XLA Modules:
  0.0 76.4 jit_solution(14312538592603451620)
XLA Ops:
  0.0 0.8 %select_reduce_fusion.1 = s32[4]{0:T(128)S(1)} fusion(s32[4]{0:T(128)} %param.8), kind=kLoop, calls=%fused_computation.7 | loop fusion | flops 44 | bytes 32 | tf_op jit(solution)/shard_map/reduce_sum | solution.py:19
  0.8 0.7 select_reduce_fusion
  1.5 0.1 copy.11
  1.7 0.3 fusion
  2.0 0.1 pad_maximum_fusion
  2.1 0.0 copy-start
  2.1 1.0 %copy-done = bf16[1,128,2048]{2,1,0:T(8,128)(2,1)S(1)} copy-done((bf16[1,128,2048]{2,1,0:T(8,128)(2,1)S(1)}, bf16[1,128,2048]{2,1,0:T(8,128)(2,1)}, u32[]{:S(2)}) %copy-start) | copy-done | bytes 524312
  3.1 0.0 copy-start.1
  3.1 0.7 copy-done.1
  3.8 71.7 %shard_map.73 = bf16[128,2048]{1,0:T(8,128)(2,1)S(1)} custom-call(bf16[128,2048]{1,0:T(8,128)(2,1)S(1)} %bitcast.8, s32[128,1]{1,0:T(8,128)S(1)} %add_subtract_fusion.off_ref, f32[128,128]{1,0:T(8,128)S(1)} %get-tuple-element.8.cos_ref, f32[128,128]{1,0:T(8,128)S(1)} %get-tuple-element.9.sin_ref, bf16[1,2048]{1,0:T(2,128)(2,1)S(1)} %copy-done.1, ...), custom_call_target="tpu_custom_call" | custom-call | tf_op jit(solution)/shard_map/pallas_call | solution.py:305
  75.6 0.8 %copy.13 = bf16[1,1,128,2048]{3,2,1,0:T(8,128)(2,1)} copy(bf16[1,1,128,2048]{3,2,1,0:T(8,128)(2,1)S(1)} %bitcast.7) | data formatting | bytes 1048576
  (4 shorter events, 0.0 us)
Async XLA Ops:
  2.1 1.0 %copy-start = (bf16[1,128,2048]{2,1,0:T(8,128)(2,1)S(1)}, bf16[1,128,2048]{2,1,0:T(8,128)(2,1)}, u32[]{:S(2)}) copy-start(bf16[1,128,2048]{2,1,0:T(8,128)(2,1)} %param.7) | copy-start | bytes 1572868
  3.1 0.7 copy-start.1
